TPU v7x, 32 devices: a whole 2x2x4 slice. The times are simulated.
32 devices in a mesh: lon: 8 (over z, y), lat: 4 (over x, core).
Axes of the slice: x: 2, y: 2, z: 4, core: 2. Of those that a mesh axis runs over, the one named last changes fastest.
Arguments:
- obs_values: bfloat16 [16384, 128], P(('lon', 'lat')), may hold values from -6 to 6
- obs_owner: int32 [16384, 1], P(('lon', 'lat')), may hold values from 0 to 7; in each aligned block of 512 rows (0 to 511, 512 to 1023, ...) at most 128 rows name the same one
- obs_cell: int32 [16384], P(('lon', 'lat')), may hold values from 0 to 2047
- obs_count: int32 [32], P(('lon', 'lat')), may hold values from 256 to 512, as said below
- obs_map: bfloat16 [128, 384], replicated, may hold values from -0.5 to 0.5
- column_mix: float32 [384, 384], replicated, may hold values from -0.3125 to 0.3125
- center: float32 [128, 512], P('lon', 'lat'), may hold values from 0.4 to 1
- neighbor: float32 [4, 128, 512], P(None, 'lon', 'lat'), may hold values from 0.08 to 0.3
Outputs:
- gradient: float32 [384, 128, 512], P(None, 'lon', 'lat')
Inputs may be any that keep to these rules, and one draw needn't show every extreme that they name: `obs_owner`: among the rows of one device at most 128 name the same longitude block, and some block is named by exactly 128 of them. `obs_count`: rows of a device past its count are not live; some device has all 512 rows live.
All inputs are finite; a program needn't handle non-finite values.
Results may differ from a plain program's by a relative error of at most 0.0029.
Values may be sent and summed in bfloat16 or wider, within the bound.
A program may use at most 64 MiB of HBM per device.

v0:
```python
import jax
import jax.numpy as jnp
from jax import lax
from jax.sharding import PartitionSpec as P

STEPS = 2


def with_halo(x, sides, width, wrap):
    for axis, dim in sides:
        size, length = (lax.axis_size(axis), x.shape[dim])
        up = [(i, (i + 1) % size) for i in range(size if wrap else size - 1)]
        down = [(j, i) for i, j in up]
        last = lax.slice_in_dim(x, length - width, length, axis=dim)
        first = lax.slice_in_dim(x, 0, width, axis=dim)
        before = lax.ppermute(last, axis, up)
        after = lax.ppermute(first, axis, down)
        x = jnp.concatenate([before, x, after], axis=dim)
    return x


def stencil(spread, middle, weights):
    return (
        middle * spread[:, 1:-1, 1:-1]
        + weights[0] * spread[:, :-2, 1:-1]
        + weights[1] * spread[:, 2:, 1:-1]
        + weights[2] * spread[:, 1:-1, :-2]
        + weights[3] * spread[:, 1:-1, 2:]
    )


def column_apply(mixing, adjoint):
    extent, lon_cells, lat_cells = adjoint.shape
    flat_cols = adjoint.reshape(extent, lon_cells * lat_cells)
    result = lax.dot_general(
        mixing,
        flat_cols,
        (((0,), (0,)), ((), ())),
        precision=lax.Precision.HIGHEST,
        preferred_element_type=jnp.float32,
    )
    return result.reshape(extent, lon_cells, lat_cells)


def on_device(obs_values, obs_owner, obs_cell, obs_count, obs_map, column_mix, center, neighbor):
    lon_count = lax.axis_size("lon")
    row_count = obs_values.shape[0]
    extent = column_mix.shape[0]
    capacity = 2 * row_count // lon_count
    slot_count = lon_count * capacity
    lon_cells, lat_cells = center.shape
    cell_count = lon_cells * lat_cells
    owners = obs_owner[:, 0]
    living = jnp.arange(row_count, dtype=jnp.int32) < obs_count[0]
    matches = (owners[:, None] == jnp.arange(lon_count, dtype=jnp.int32)[None, :]).astype(jnp.int32)
    earlier = jnp.sum(jnp.cumsum(matches, axis=0) * matches, axis=1) - 1
    target = owners * capacity + earlier
    places = jnp.where(living, obs_cell, -1)
    slot_places = (
        jnp.full((slot_count,), -1, jnp.int32).at[target].set(places).reshape(lon_count, capacity)
    )
    packed = (
        jnp.zeros((slot_count, extent), jnp.bfloat16)
        .at[target]
        .set(jnp.dot(obs_values, obs_map, preferred_element_type=jnp.float32).astype(jnp.bfloat16))
    )
    packed = packed.reshape(lon_count, capacity, extent)
    arrived, labels = (
        lax.all_to_all(packed, "lon", split_axis=0, concat_axis=0, tiled=True),
        lax.all_to_all(slot_places, "lon", split_axis=0, concat_axis=0, tiled=True),
    )
    block_rows = min(512, slot_count)
    batched = arrived.reshape(slot_count // block_rows, block_rows, extent)
    batched_places = labels.reshape(slot_count // block_rows, block_rows)
    targets = jnp.arange(cell_count, dtype=jnp.int32)

    def accumulate(running, element):
        values, places_in = element
        onehot = (places_in[:, None] == targets[None, :]).astype(jnp.bfloat16)
        update = lax.dot_general(
            values, onehot, (((0,), (0,)), ((), ())), preferred_element_type=jnp.float32
        )
        return (running + update, None)

    forcing, unused = lax.scan(
        accumulate, jnp.zeros((extent, cell_count), jnp.float32), (batched, batched_places)
    )
    adjoint = forcing.reshape(extent, lon_cells, lat_cells)
    for section in range(STEPS):
        mixed = column_apply(column_mix, adjoint)
        spread = with_halo(mixed, (("lon", 1),), 1, True)
        spread = with_halo(spread, (("lat", 2),), 1, False)
        adjoint = stencil(spread, center, neighbor)
    return adjoint


def solution(mesh):
    return jax.shard_map(
        on_device,
        mesh=mesh,
        in_specs=(
            P(("lon", "lat"), None),
            P(("lon", "lat"), None),
            P(("lon", "lat")),
            P(("lon", "lat")),
            P(),
            P(),
            P("lon", "lat"),
            P(None, "lon", "lat"),
        ),
        out_specs=P(None, "lon", "lat"),
        check_vma=False,
    )
```

profile of v0, /device:TPU:1, one launch (start us, length us, event | category | flops | bytes accessed | tf_op | source)
XLA Modules:
  0.0 137.6 jit_solution(2249607796687000426)
XLA Ops:
  0.0 0.7 fusion.26
  0.8 1.1 reduce-window.6
  1.9 0.2 slice_reduce_fusion
  2.1 0.8 fusion.25
  2.9 0.7 compare_select_fusion
  4.3 0.7 fusion.29
  4.9 3.0 %scatter_custom_fusion.1 = s32[1024]{0:T(1024)} fusion(s32[512]{0:T(512)S(1)} %bitcast.56, s32[512]{0:T(512)S(1)} %fusion.29, s32[]{:T(128)} %constant.17.clone.1), kind=kCustom, calls=%fused_computation.52 | custom fusion | bytes 4100 | tf_op jit(solution)/shard_map/scatter | solution.py:60
  8.0 6.4 %all-to-all-start.1 = ((s32[8,1,128]{2,1,0:T(1,128)}), s32[8,1,128]{2,1,0:T(1,128)S(1)}, u32[]{:S(2)}, u32[]{:S(2)}) async-start(s32[8,1,128]{2,1,0:T(1,128)} %bitcast.9), calls=%async_computation.1 | async-start | bytes 8192 | tf_op jit(solution)/shard_map/all_to_all | solution.py:70
  14.3 1.2 convolution_convert_fusion
  15.5 3.3 %scatter_custom_fusion = bf16[1024,384]{1,0:T(8,128)(2,1)} fusion(s32[512]{0:T(512)S(1)} %bitcast.57, bf16[512,384]{1,0:T(8,128)(2,1)S(1)} %convolution_convert_fusion, bf16[]{:T(256)} %constant.14.clone.1), kind=kCustom, calls=%fused_computation.38 | custom fusion | bytes 786434 | tf_op jit(solution)/shard_map/scatter | solution.py:65
  18.9 0.7 all-to-all-done.1
  19.6 4.7 %all-to-all-start = ((bf16[8,128,384]{2,1,0:T(8,128)(2,1)}), bf16[8,128,384]{2,1,0:T(8,128)(2,1)S(1)}, u32[]{:S(2)}, u32[]{:S(2)}) async-start(bf16[8,128,384]{2,1,0:T(8,128)(2,1)} %bitcast.6), calls=%async_computation | async-start | bytes 1572864 | tf_op jit(solution)/shard_map/all_to_all | solution.py:69
  24.3 0.5 broadcast.58
  24.8 0.6 reduce.5
  25.4 17.5 %all-to-all-done = bf16[8,128,384]{2,1,0:T(8,128)(2,1)S(1)} async-done(((bf16[8,128,384]{2,1,0:T(8,128)(2,1)}), bf16[8,128,384]{2,1,0:T(8,128)(2,1)S(1)}, u32[]{:S(2)}, u32[]{:S(2)}) %all-to-all-start) | async-done | bytes 786464 | tf_op jit(solution)/shard_map/all_to_all | solution.py:69
  42.9 7.7 %while.11 = (s32[]{:T(128)}, f32[384,2048]{1,0:T(8,128)}, bf16[2,512,384]{2,1,0:T(8,128)(2,1)S(1)}, s32[2,512]{1,0:T(2,128)S(1)}, s32[]{:T(128)}, /*index=5*/s32[]{:T(128)}) while((s32[]{:T(128)}, f32[384,2048]{1,0:T(8,128)}, bf16[2,512,384]{2,1,0:T(8,128)(2,1)S(1)}, s32[2,512]{1,0:T(2,128)S(1)}, s32[]{:T(128)}, ...), condition=%wide.region_6.7_spmd.clone, body=%wide.region_5.6_spmd.clone.sunk | while | flops 807927808 | bytes 6690911 | solution.py:85
  42.9 2.9 %select_add_fusion.2 = f32[384,2048]{1,0:T(8,128)} fusion(f32[384,2048]{1,0:T(8,128)} %get-tuple-element.102, s32[512]{0:T(512)S(1)} %bitcast.52, pred[]{:T(512)S(6)} %compare.3, bf16[2,512,384]{2,1,0:T(8,128)(2,1)S(1)} %get-tuple-element.109, s32[]{:T(128)S(6)} %copy.62), kind=kOutput, calls=%fused_computation.5.clone.1 | convolution fusion | flops 807927808 | bytes 6686725 | tf_op jit(solution)/shard_map/while/body/eval_jaxpr/dot_general | solution.py:80
  45.8 4.8 %select_add_fusion.2 = f32[384,2048]{1,0:T(8,128)} fusion(f32[384,2048]{1,0:T(8,128)} %get-tuple-element.102, s32[512]{0:T(512)S(1)} %bitcast.52, pred[]{:T(512)S(6)} %compare.3, bf16[2,512,384]{2,1,0:T(8,128)(2,1)S(1)} %get-tuple-element.109, s32[]{:T(128)S(6)} %copy.62), kind=kOutput, calls=%fused_computation.5.clone.1 | convolution fusion | flops 807927808 | bytes 6686725 | tf_op jit(solution)/shard_map/while/body/eval_jaxpr/dot_general | solution.py:80
  50.6 8.5 %fusion.34 = f32[2048,384]{1,0:T(8,128)S(1)} fusion(f32[384,2048]{1,0:T(8,128)} %get-tuple-element.32, f32[384,384]{1,0:T(8,128)S(1)} %copy-done), kind=kOutput, calls=%fused_computation.60 | convolution fusion | flops 3623878656 | bytes 6881280 | tf_op jit(solution)/shard_map/dot_general | solution.py:35
  59.1 1.7 %copy-done.1 = f32[2048,384]{1,0:T(8,128)} copy-done((f32[2048,384]{1,0:T(8,128)}, f32[2048,384]{1,0:T(8,128)S(1)}, u32[]{:S(2)}) %copy-start.1) | copy-done | bytes 3145752
  60.9 4.1 %collective-permute-start.1 = (f32[384,1,128]{2,0,1:T(8,128)S(1)}, f32[384,1,128]{2,0,1:T(8,128)S(1)}, u32[]{:S(2)}, u32[]{:S(2)}) collective-permute-start(f32[384,1,128]{2,0,1:T(8,128)S(1)} %copy.57), channel_id=1, source_target_pairs={{4,0},{8,4},{12,8},{16,12},{20,16},{24,20},{28,24},{0,28},{5,1},{9... | collective-permute-start | bytes 589832 | tf_op jit(solution)/shard_map/ppermute | solution.py:17
  65.2 0.2 collective-permute-start
  65.4 5.4 %copy.38 = f32[384,16,128]{0,1,2:T(8,128)} copy(f32[384,16,128]{0,2,1:T(8,128)} %bitcast.45) | data formatting | bytes 6291456 | tf_op jit(solution)/shard_map/reshape | solution.py:42
  70.8 0.2 copy.39
  71.0 2.8 %collective-permute-done = f32[384,1,128]{2,0,1:T(8,128)S(1)} collective-permute-done((f32[384,1,128]{2,0,1:T(8,128)S(1)}, f32[384,1,128]{2,0,1:T(8,128)S(1)}, u32[]{:S(2)}, u32[]{:S(2)}) %collective-permute-start) | collective-permute-done | bytes 196640 | tf_op jit(solution)/shard_map/ppermute | solution.py:16
  73.8 0.2 copy.37
  74.0 2.6 %pad_maximum_fusion = f32[384,18,128]{0,1,2:T(8,128)S(1)} fusion(f32[384,1,128]{0,1,2:T(1,128)S(1)} %copy.39, f32[384,16,128]{0,1,2:T(8,128)} %copy.38, f32[384,1,128]{0,1,2:T(1,128)S(1)} %copy.37), kind=kLoop, calls=%fused_computation.11 | loop fusion | flops 1769472 | bytes 7077888 | tf_op jit(solution)/shard_map/concatenate | solution.py:18
  76.6 3.6 %collective-permute-start.3 = (f32[384,18,1]{0,1,2:T(8,128)S(1)}, f32[384,18,1]{0,1,2:T(8,128)S(1)}, u32[]{:S(2)}, u32[]{:S(2)}) collective-permute-start(f32[384,18,1]{0,1,2:T(8,128)S(1)} %get-tuple-element.61), channel_id=1, source_target_pairs={{1,0},{2,1},{3,2},{5,4},{6,5},{7,6},{9,8},{10,9},{11,10},{13,12},{... | collective-permute-start | bytes 82952 | tf_op jit(solution)/shard_map/ppermute | solution.py:17
  80.1 3.0 %collective-permute-start.2 = (f32[384,18,1]{0,1,2:T(8,128)S(1)}, f32[384,18,1]{0,1,2:T(8,128)S(1)}, u32[]{:S(2)}, u32[]{:S(2)}) collective-permute-start(f32[384,18,1]{0,1,2:T(8,128)S(1)} %get-tuple-element.60), channel_id=1, source_target_pairs={{0,1},{1,2},{2,3},{4,5},{5,6},{6,7},{8,9},{9,10},{10,11},{12,13},{... | collective-permute-start | bytes 82952 | tf_op jit(solution)/shard_map/ppermute | solution.py:16
  83.2 2.4 %copy.41 = f32[384,18,128]{0,2,1:T(8,128)} copy(f32[384,18,128]{0,1,2:T(8,128)S(1)} %pad_maximum_fusion) | data formatting | bytes 7077888 | tf_op jit(solution)/shard_map/concatenate | solution.py:18
  85.6 0.1 copy.36
  85.7 0.1 copy.34
  85.9 7.9 %fusion.16 = f32[384,16,128]{0,2,1:T(8,128)S(1)} fusion(f32[384,18,1]{0,2,1:T(1,128)S(1)} %copy.43, f32[384,18,128]{0,2,1:T(8,128)} %copy.41, f32[384,18,1]{0,2,1:T(1,128)S(1)} %copy.40, f32[384,1,128]{0,2,1:T(8,128)S(1)} %copy.36, f32[384,16,128]{0,2,1:T(8,128)} %bitcast.46, f32[384,1,128]{0,2,1:T(8,128)S(1)} %copy.34, f32[16,128]{1,0:T(8,128)S(1)} %get-tuple-element.68, ...), kind=kLoop, calls=%fused_computation.27 | loop fusion | flops 10223616 | bytes 10319872 | tf_op jit(solution)/shard_map/add | solution.py:24
  93.8 6.7 %fusion.35 = f32[2048,384]{1,0:T(8,128)S(1)} fusion(f32[384,2048]{0,1:T(8,128)S(1)} %bitcast.50, f32[384,384]{1,0:T(8,128)S(1)} %copy-done), kind=kOutput, calls=%fused_computation.61 | convolution fusion | flops 3623878656 | bytes 6881280 | tf_op jit(solution)/shard_map/dot_general | solution.py:35
  100.5 1.7 %copy-done.2 = f32[2048,384]{1,0:T(8,128)} copy-done((f32[2048,384]{1,0:T(8,128)}, f32[2048,384]{1,0:T(8,128)S(1)}, u32[]{:S(2)}) %copy-start.2) | copy-done | bytes 3145752
  102.4 1.6 %collective-permute-start.5 = (f32[384,1,128]{2,0,1:T(8,128)S(1)}, f32[384,1,128]{2,0,1:T(8,128)S(1)}, u32[]{:S(2)}, u32[]{:S(2)}) collective-permute-start(f32[384,1,128]{2,0,1:T(8,128)S(1)} %copy.59), channel_id=1, source_target_pairs={{4,0},{8,4},{12,8},{16,12},{20,16},{24,20},{28,24},{0,28},{5,1},{9... | collective-permute-start | bytes 589832 | tf_op jit(solution)/shard_map/ppermute | solution.py:17
  104.1 0.3 collective-permute-start.4
  104.4 5.4 %copy.49 = f32[384,16,128]{0,1,2:T(8,128)} copy(f32[384,16,128]{0,2,1:T(8,128)} %bitcast.48) | data formatting | bytes 6291456 | tf_op jit(solution)/shard_map/reshape | solution.py:42
  109.7 0.2 copy.50
  109.9 3.9 %collective-permute-done.4 = f32[384,1,128]{2,0,1:T(8,128)S(1)} collective-permute-done((f32[384,1,128]{2,0,1:T(8,128)S(1)}, f32[384,1,128]{2,0,1:T(8,128)S(1)}, u32[]{:S(2)}, u32[]{:S(2)}) %collective-permute-start.4) | collective-permute-done | bytes 196640 | tf_op jit(solution)/shard_map/ppermute | solution.py:16
  113.8 0.2 copy.48
  114.0 2.6 %pad_maximum_fusion.1 = f32[384,18,128]{0,1,2:T(8,128)S(1)} fusion(f32[384,1,128]{0,1,2:T(1,128)S(1)} %copy.50, f32[384,16,128]{0,1,2:T(8,128)} %copy.49, f32[384,1,128]{0,1,2:T(1,128)S(1)} %copy.48), kind=kLoop, calls=%fused_computation.12 | loop fusion | flops 1769472 | bytes 7077888 | tf_op jit(solution)/shard_map/concatenate | solution.py:18
  116.6 2.5 %collective-permute-start.7 = (f32[384,18,1]{0,1,2:T(8,128)S(1)}, f32[384,18,1]{0,1,2:T(8,128)S(1)}, u32[]{:S(2)}, u32[]{:S(2)}) collective-permute-start(f32[384,18,1]{0,1,2:T(8,128)S(1)} %get-tuple-element.59), channel_id=1, source_target_pairs={{1,0},{2,1},{3,2},{5,4},{6,5},{7,6},{9,8},{10,9},{11,10},{13,12},{... | collective-permute-start | bytes 82952 | tf_op jit(solution)/shard_map/ppermute | solution.py:17
  119.1 3.1 %collective-permute-start.6 = (f32[384,18,1]{0,1,2:T(8,128)S(1)}, f32[384,18,1]{0,1,2:T(8,128)S(1)}, u32[]{:S(2)}, u32[]{:S(2)}) collective-permute-start(f32[384,18,1]{0,1,2:T(8,128)S(1)} %get-tuple-element.58), channel_id=1, source_target_pairs={{0,1},{1,2},{2,3},{4,5},{5,6},{6,7},{8,9},{9,10},{10,11},{12,13},{... | collective-permute-start | bytes 82952 | tf_op jit(solution)/shard_map/ppermute | solution.py:16
  122.2 2.4 %copy.52 = f32[384,18,128]{0,2,1:T(8,128)} copy(f32[384,18,128]{0,1,2:T(8,128)S(1)} %pad_maximum_fusion.1) | data formatting | bytes 7077888 | tf_op jit(solution)/shard_map/concatenate | solution.py:18
  124.7 0.1 copy.45
  124.9 9.1 %fusion.8 = f32[384,16,128]{0,2,1:T(8,128)} fusion(f32[384,18,1]{0,2,1:T(1,128)S(1)} %copy.54, f32[384,18,128]{0,2,1:T(8,128)} %copy.52, f32[384,18,1]{0,2,1:T(1,128)S(1)} %copy.51, f32[384,1,128]{0,2,1:T(8,128)S(1)} %copy.47, f32[384,16,128]{0,2,1:T(8,128)} %bitcast.49, f32[384,1,128]{0,2,1:T(8,128)S(1)} %copy.45, f32[16,128]{1,0:T(8,128)S(1)} %get-tuple-element.68, ...), kind=kLoop, calls=%fused_computation.15 | loop fusion | flops 10223616 | bytes 10319872 | tf_op jit(solution)/shard_map/add | solution.py:24
  134.0 3.5 %copy.55 = f32[384,16,128]{2,1,0:T(8,128)} copy(f32[384,16,128]{0,2,1:T(8,128)} %fusion.8) | data formatting | bytes 6291456 | tf_op jit(solution)/shard_map/add | solution.py:24
  (35 shorter events, 0.9 us)
Async XLA Ops:
  0.0 50.6 %copy-start = (f32[384,384]{1,0:T(8,128)S(1)}, f32[384,384]{1,0:T(8,128)}, u32[]{:S(2)}) copy-start(f32[384,384]{1,0:T(8,128)} %param.15) | copy-start | bytes 1769476
  8.0 11.6 %all-to-all-start.1 = ((s32[8,1,128]{2,1,0:T(1,128)}), s32[8,1,128]{2,1,0:T(1,128)S(1)}, u32[]{:S(2)}, u32[]{:S(2)}) async-start(s32[8,1,128]{2,1,0:T(1,128)} %bitcast.9), calls=%async_computation.1 | async-start | bytes 8192 | tf_op jit(solution)/shard_map/all_to_all | solution.py:70
  19.6 23.3 %all-to-all-start = ((bf16[8,128,384]{2,1,0:T(8,128)(2,1)}), bf16[8,128,384]{2,1,0:T(8,128)(2,1)S(1)}, u32[]{:S(2)}, u32[]{:S(2)}) async-start(bf16[8,128,384]{2,1,0:T(8,128)(2,1)} %bitcast.6), calls=%async_computation | async-start | bytes 1572864 | tf_op jit(solution)/shard_map/all_to_all | solution.py:69
  59.1 1.7 %copy-start.1 = (f32[2048,384]{1,0:T(8,128)}, f32[2048,384]{1,0:T(8,128)S(1)}, u32[]{:S(2)}) copy-start(f32[2048,384]{1,0:T(8,128)S(1)} %fusion.34) | copy-start | bytes 9437188
  60.9 9.9 %collective-permute-start.1 = (f32[384,1,128]{2,0,1:T(8,128)S(1)}, f32[384,1,128]{2,0,1:T(8,128)S(1)}, u32[]{:S(2)}, u32[]{:S(2)}) collective-permute-start(f32[384,1,128]{2,0,1:T(8,128)S(1)} %copy.57), channel_id=1, source_target_pairs={{4,0},{8,4},{12,8},{16,12},{20,16},{24,20},{28,24},{0,28},{5,1},{9... | collective-permute-start | bytes 589832 | tf_op jit(solution)/shard_map/ppermute | solution.py:17
  65.2 8.6 %collective-permute-start = (f32[384,1,128]{2,0,1:T(8,128)S(1)}, f32[384,1,128]{2,0,1:T(8,128)S(1)}, u32[]{:S(2)}, u32[]{:S(2)}) collective-permute-start(f32[384,1,128]{2,0,1:T(8,128)S(1)} %copy.56), channel_id=1, source_target_pairs={{0,4},{4,8},{8,12},{12,16},{16,20},{20,24},{24,28},{28,0},{1,5},{5... | collective-permute-start | bytes 589832 | tf_op jit(solution)/shard_map/ppermute | solution.py:16
  73.9 9.2 %copy-start.4 = (f32[4,16,128]{2,1,0:T(8,128)S(1)}, f32[4,16,128]{2,1,0:T(8,128)}, u32[]{:S(2)}) copy-start(f32[4,16,128]{2,1,0:T(8,128)} %param.17) | copy-start | bytes 98308
  76.6 9.3 %collective-permute-start.3 = (f32[384,18,1]{0,1,2:T(8,128)S(1)}, f32[384,18,1]{0,1,2:T(8,128)S(1)}, u32[]{:S(2)}, u32[]{:S(2)}) collective-permute-start(f32[384,18,1]{0,1,2:T(8,128)S(1)} %get-tuple-element.61), channel_id=1, source_target_pairs={{1,0},{2,1},{3,2},{5,4},{6,5},{7,6},{9,8},{10,9},{11,10},{13,12},{... | collective-permute-start | bytes 82952 | tf_op jit(solution)/shard_map/ppermute | solution.py:17
  80.1 5.8 %collective-permute-start.2 = (f32[384,18,1]{0,1,2:T(8,128)S(1)}, f32[384,18,1]{0,1,2:T(8,128)S(1)}, u32[]{:S(2)}, u32[]{:S(2)}) collective-permute-start(f32[384,18,1]{0,1,2:T(8,128)S(1)} %get-tuple-element.60), channel_id=1, source_target_pairs={{0,1},{1,2},{2,3},{4,5},{5,6},{6,7},{8,9},{9,10},{10,11},{12,13},{... | collective-permute-start | bytes 82952 | tf_op jit(solution)/shard_map/ppermute | solution.py:16
  83.2 2.8 %copy-start.3 = (f32[16,128]{1,0:T(8,128)S(1)}, f32[16,128]{1,0:T(8,128)}, u32[]{:S(2)}) copy-start(f32[16,128]{1,0:T(8,128)} %param.16) | copy-start | bytes 24580
  100.5 1.7 %copy-start.2 = (f32[2048,384]{1,0:T(8,128)}, f32[2048,384]{1,0:T(8,128)S(1)}, u32[]{:S(2)}) copy-start(f32[2048,384]{1,0:T(8,128)S(1)} %fusion.35) | copy-start | bytes 9437188
  102.4 7.4 %collective-permute-start.5 = (f32[384,1,128]{2,0,1:T(8,128)S(1)}, f32[384,1,128]{2,0,1:T(8,128)S(1)}, u32[]{:S(2)}, u32[]{:S(2)}) collective-permute-start(f32[384,1,128]{2,0,1:T(8,128)S(1)} %copy.59), channel_id=1, source_target_pairs={{4,0},{8,4},{12,8},{16,12},{20,16},{24,20},{28,24},{0,28},{5,1},{9... | collective-permute-start | bytes 589832 | tf_op jit(solution)/shard_map/ppermute | solution.py:17
  104.1 9.7 %collective-permute-start.4 = (f32[384,1,128]{2,0,1:T(8,128)S(1)}, f32[384,1,128]{2,0,1:T(8,128)S(1)}, u32[]{:S(2)}, u32[]{:S(2)}) collective-permute-start(f32[384,1,128]{2,0,1:T(8,128)S(1)} %copy.58), channel_id=1, source_target_pairs={{0,4},{4,8},{8,12},{12,16},{16,20},{20,24},{24,28},{28,0},{1,5},{5... | collective-permute-start | bytes 589832 | tf_op jit(solution)/shard_map/ppermute | solution.py:16
  116.6 8.2 %collective-permute-start.7 = (f32[384,18,1]{0,1,2:T(8,128)S(1)}, f32[384,18,1]{0,1,2:T(8,128)S(1)}, u32[]{:S(2)}, u32[]{:S(2)}) collective-permute-start(f32[384,18,1]{0,1,2:T(8,128)S(1)} %get-tuple-element.59), channel_id=1, source_target_pairs={{1,0},{2,1},{3,2},{5,4},{6,5},{7,6},{9,8},{10,9},{11,10},{13,12},{... | collective-permute-start | bytes 82952 | tf_op jit(solution)/shard_map/ppermute | solution.py:17
  119.1 5.8 %collective-permute-start.6 = (f32[384,18,1]{0,1,2:T(8,128)S(1)}, f32[384,18,1]{0,1,2:T(8,128)S(1)}, u32[]{:S(2)}, u32[]{:S(2)}) collective-permute-start(f32[384,18,1]{0,1,2:T(8,128)S(1)} %get-tuple-element.58), channel_id=1, source_target_pairs={{0,1},{1,2},{2,3},{4,5},{5,6},{6,7},{8,9},{9,10},{10,11},{12,13},{... | collective-permute-start | bytes 82952 | tf_op jit(solution)/shard_map/ppermute | solution.py:16
where the time goes:
time: 138 us
  local copies, waits for them, and re-layouts  31.3 us (23%)
  starting transfers between devices  29.5 us (21%)
  other arithmetic  26.8 us (19%)
  waiting for transfers between devices  25 us (18%)
  matrix products  24.1 us (17%)
    all_to_all x1, waiting for transfers between devices, on_device(): lax.all_to_all(packed, 'lon', split_axis=0, concat_axis=0, tiled=True)  17.5 us
    add x2, other arithmetic, stencil(): middle * spread[:, 1:-1, 1:-1] + weights[0] * spread[:, :-2, 1:-1]  17 us
    dot_general x2, matrix products, column_apply(): lax.dot_general(mixing, flat_cols, (((0,), (0,)), ((), ())), precision=la...  15.2 us
    ppermute x4, starting transfers between devices, with_halo(): after = lax.ppermute(first, axis, down)  11.7 us
    reshape x2, local copies, waits for them, and re-layouts, column_apply(): return result.reshape(extent, lon_cells, lat_cells)  10.7 us
    dot_general x2, matrix products, accumulate(): lax.dot_general(values, onehot, (((0,), (0,)), ((), ())), preferred_eleme...  7.72 us
    ppermute x4, waiting for transfers between devices, with_halo(): before = lax.ppermute(last, axis, up)  6.75 us
    ppermute x4, starting transfers between devices, with_halo(): before = lax.ppermute(last, axis, up)  6.63 us
  transfers between devices with their start and end apart: 10, of which 4 were waited for; matrix products, arithmetic and copies ran while one was open for 16% of the time, Pallas kernels for 0%

commit v1 on v0

--- a/solution.py
+++ b/solution.py
@@ -4,6 +4,22 @@
 from jax.sharding import PartitionSpec as P
 
 STEPS = 2
+
+
+def exchange_in_pairs(array, axis, split, join):
+    ways, here = (lax.axis_size(axis), lax.axis_index(axis))
+    width = array.shape[split] // ways
+    dims = list(array.shape)
+    dims[split] = width
+    height = dims[join]
+    dims[join] = height * ways
+    full = jnp.zeros(dims, array.dtype)
+    for mask in range(ways):
+        part = lax.dynamic_slice_in_dim(array, (here ^ mask) * width, width, axis=split)
+        if mask:
+            part = lax.ppermute(part, axis, [(d, d ^ mask) for d in range(ways)])
+        full = lax.dynamic_update_slice_in_dim(full, part, (here ^ mask) * height, axis=join)
+    return full
 
 
 def with_halo(x, sides, width, wrap):
@@ -67,7 +83,7 @@
     packed = packed.reshape(lon_count, capacity, extent)
     arrived, labels = (
         lax.all_to_all(packed, "lon", split_axis=0, concat_axis=0, tiled=True),
-        lax.all_to_all(slot_places, "lon", split_axis=0, concat_axis=0, tiled=True),
+        exchange_in_pairs(slot_places, "lon", 0, 0),
     )
     block_rows = min(512, slot_count)
     batched = arrived.reshape(slot_count // block_rows, block_rows, extent)

time: 138 us -> 129 us (0.935)
  waiting for transfers between devices: 25 us -> 10 us
  starting transfers between devices: 29.5 us -> 37.5 us
  other arithmetic: 26.8 us -> 25.4 us
    all_to_all x1, waiting for transfers between devices: 17.5 us -> 0.01 us  [on_device(): lax.all_to_all(packed, 'lon', split_axis=0, concat_axis=0, tiled=True)]
    ppermute x0 -> x7, starting transfers between devices: none -> 13 us  [exchange_in_pairs(): part = lax.ppermute(part, axis, [(d, d ^ mask) for d in range(ways)])]
    all_to_all x1 -> x0, starting transfers between devices: 6.38 us -> none  [on_device(): lax.all_to_all(slot_places, 'lon', split_axis=0, concat_axis=0, tiled=True)]
    ppermute x0 -> x7, waiting for transfers between devices: none -> 3.89 us  [exchange_in_pairs(): part = lax.ppermute(part, axis, [(d, d ^ mask) for d in range(ways)])]
    all_to_all x1, starting transfers between devices: 4.72 us -> 6.38 us  [on_device(): lax.all_to_all(packed, 'lon', split_axis=0, concat_axis=0, tiled=True)]
    unnamed x14 -> x16, local copies, waits for them, and re-layouts: 3.82 us -> 3.82 us
  transfers between devices with their start and end apart: 10 -> 16, of which waited for: 4 -> 4; matrix products, arithmetic and copies ran while one was open for 16% -> 15% of each run, Pallas kernels for 0% -> 0%
where the time goes in v1:
time: 129 us
  starting transfers between devices  37.5 us (29%)
  local copies, waits for them, and re-layouts  30.6 us (24%)
  other arithmetic  25.4 us (20%)
  matrix products  24.1 us (19%)
  waiting for transfers between devices  10 us (8%)
    add x2, other arithmetic, stencil(): middle * spread[:, 1:-1, 1:-1] + weights[0] * spread[:, :-2, 1:-1]  16.8 us
    dot_general x2, matrix products, column_apply(): lax.dot_general(mixing, flat_cols, (((0,), (0,)), ((), ())), precision=la...  15.2 us
    ppermute x7, starting transfers between devices, exchange_in_pairs(): part = lax.ppermute(part, axis, [(d, d ^ mask) for d in range(ways)])  13 us
    ppermute x4, starting transfers between devices, with_halo(): after = lax.ppermute(first, axis, down)  11.6 us
    reshape x2, local copies, waits for them, and re-layouts, column_apply(): return result.reshape(extent, lon_cells, lat_cells)  10.7 us
    dot_general x2, matrix products, accumulate(): lax.dot_general(values, onehot, (((0,), (0,)), ((), ())), preferred_eleme...  7.72 us
    ppermute x4, starting transfers between devices, with_halo(): before = lax.ppermute(last, axis, up)  6.47 us
    all_to_all x1, starting transfers between devices, on_device(): lax.all_to_all(packed, 'lon', split_axis=0, concat_axis=0, tiled=True)  6.38 us
  transfers between devices with their start and end apart: 16, of which 4 were waited for; matrix products, arithmetic and copies ran while one was open for 15% of the time, Pallas kernels for 0%

profile of v1, /device:TPU:1, one launch (start us, length us, event | category | flops | bytes accessed | tf_op | source)
XLA Modules:
  0.0 128.7 jit_solution(10752246021187578912)
XLA Ops:
  0.0 0.8 fusion.26
  0.8 1.1 reduce-window.6
  1.9 0.2 slice_reduce_fusion
  2.2 0.8 fusion.25
  2.9 0.7 compare_select_fusion
  3.6 1.2 convolution_convert_fusion
  4.8 3.3 %scatter_custom_fusion = bf16[1024,384]{1,0:T(8,128)(2,1)} fusion(s32[512]{0:T(512)S(1)} %bitcast.57, bf16[512,384]{1,0:T(8,128)(2,1)S(1)} %convolution_convert_fusion, bf16[]{:T(256)} %constant.9.clone.1), kind=kCustom, calls=%fused_computation.38 | custom fusion | bytes 786434 | tf_op jit(solution)/shard_map/scatter | solution.py:81
  8.2 6.4 %all-to-all-start = ((bf16[8,128,384]{2,1,0:T(8,128)(2,1)}), bf16[8,128,384]{2,1,0:T(8,128)(2,1)S(1)}, u32[]{:S(2)}, u32[]{:S(2)}) async-start(bf16[8,128,384]{2,1,0:T(8,128)(2,1)} %bitcast.6), calls=%async_computation | async-start | bytes 1572864 | tf_op jit(solution)/shard_map/all_to_all | solution.py:85
  15.2 2.4 %scatter_custom_fusion.1 = s32[1024]{0:T(1024)S(1)} fusion(s32[512]{0:T(512)S(1)} %bitcast.58, s32[512]{0:T(512)S(1)} %fusion.29, s32[]{:T(128)} %constant.10.clone.1), kind=kCustom, calls=%fused_computation.52 | custom fusion | bytes 4100 | tf_op jit(solution)/shard_map/scatter | solution.py:76
  17.7 1.5 %collective-permute-start = (s32[1,128]{1,0:T(1,128)S(1)}, s32[1,128]{1,0:T(1,128)S(1)}, u32[]{:S(2)}, u32[]{:S(2)}) collective-permute-start(s32[1,128]{1,0:T(1,128)S(1)} %get-tuple-element.76), channel_id=1, source_target_pairs={{0,4},{4,0},{8,12},{12,8},{16,20},{20,16},{24,28},{28,24},{1,5},{5... | collective-permute-start | bytes 1544 | tf_op jit(solution)/shard_map/ppermute | solution.py:20
  19.3 1.2 collective-permute-start.1
  20.5 2.3 %collective-permute-start.3 = (s32[1,128]{1,0:T(1,128)S(1)}, s32[1,128]{1,0:T(1,128)S(1)}, u32[]{:S(2)}, u32[]{:S(2)}) collective-permute-start(s32[1,128]{1,0:T(1,128)S(1)} %get-tuple-element.73), channel_id=1, source_target_pairs={{0,16},{4,20},{8,24},{12,28},{16,0},{20,4},{24,8},{28,12},{1,17},{... | collective-permute-start | bytes 1544 | tf_op jit(solution)/shard_map/ppermute | solution.py:20
  22.8 1.2 collective-permute-start.4
  24.0 3.0 %collective-permute-start.5 = (s32[1,128]{1,0:T(1,128)S(1)}, s32[1,128]{1,0:T(1,128)S(1)}, u32[]{:S(2)}, u32[]{:S(2)}) collective-permute-start(s32[1,128]{1,0:T(1,128)S(1)} %get-tuple-element.71), channel_id=1, source_target_pairs={{0,24},{4,28},{8,16},{12,20},{16,8},{20,12},{24,0},{28,4},{1,25},{... | collective-permute-start | bytes 1544 | tf_op jit(solution)/shard_map/ppermute | solution.py:20
  27.1 3.7 %collective-permute-start.6 = (s32[1,128]{1,0:T(1,128)S(1)}, s32[1,128]{1,0:T(1,128)S(1)}, u32[]{:S(2)}, u32[]{:S(2)}) collective-permute-start(s32[1,128]{1,0:T(1,128)S(1)} %get-tuple-element.70), channel_id=1, source_target_pairs={{0,28},{4,24},{8,20},{12,16},{16,12},{20,8},{24,4},{28,0},{1,29},{... | collective-permute-start | bytes 1544 | tf_op jit(solution)/shard_map/ppermute | solution.py:20
  30.9 2.8 %collective-permute-done.3 = s32[1,128]{1,0:T(1,128)S(1)} collective-permute-done((s32[1,128]{1,0:T(1,128)S(1)}, s32[1,128]{1,0:T(1,128)S(1)}, u32[]{:S(2)}, u32[]{:S(2)}) %collective-permute-start.3) | collective-permute-done | bytes 544 | tf_op jit(solution)/shard_map/ppermute | solution.py:20
  33.7 1.1 collective-permute-done.4
  34.9 0.2 dynamic_update_slice.31
  35.1 7.8 %while.11 = (s32[]{:T(128)}, f32[384,2048]{1,0:T(8,128)}, bf16[2,512,384]{2,1,0:T(8,128)(2,1)S(1)}, s32[2,512]{1,0:T(2,128)S(1)}, s32[]{:T(128)}, /*index=5*/s32[]{:T(128)}) while((s32[]{:T(128)}, f32[384,2048]{1,0:T(8,128)}, bf16[2,512,384]{2,1,0:T(8,128)(2,1)S(1)}, s32[2,512]{1,0:T(2,128)S(1)}, s32[]{:T(128)}, ...), condition=%wide.region_6.7_spmd.clone, body=%wide.region_5.6_spmd.clone.sunk | while | flops 807927808 | bytes 6690911 | solution.py:101
  35.1 2.9 %select_add_fusion.2 = f32[384,2048]{1,0:T(8,128)} fusion(f32[384,2048]{1,0:T(8,128)} %get-tuple-element.110, s32[512]{0:T(512)S(1)} %bitcast.52, pred[]{:T(512)S(6)} %compare.3, bf16[2,512,384]{2,1,0:T(8,128)(2,1)S(1)} %get-tuple-element.117, s32[]{:T(128)S(6)} %copy.70), kind=kOutput, calls=%fused_computation.5.clone.1 | convolution fusion | flops 807927808 | bytes 6686725 | tf_op jit(solution)/shard_map/while/body/eval_jaxpr/dot_general | solution.py:96
  38.1 4.8 %select_add_fusion.2 = f32[384,2048]{1,0:T(8,128)} fusion(f32[384,2048]{1,0:T(8,128)} %get-tuple-element.110, s32[512]{0:T(512)S(1)} %bitcast.52, pred[]{:T(512)S(6)} %compare.3, bf16[2,512,384]{2,1,0:T(8,128)(2,1)S(1)} %get-tuple-element.117, s32[]{:T(128)S(6)} %copy.70), kind=kOutput, calls=%fused_computation.5.clone.1 | convolution fusion | flops 807927808 | bytes 6686725 | tf_op jit(solution)/shard_map/while/body/eval_jaxpr/dot_general | solution.py:96
  42.9 8.5 %fusion.34 = f32[2048,384]{1,0:T(8,128)S(1)} fusion(f32[384,2048]{1,0:T(8,128)} %get-tuple-element.32, f32[384,384]{1,0:T(8,128)S(1)} %copy-done), kind=kOutput, calls=%fused_computation.68 | convolution fusion | flops 3623878656 | bytes 6881280 | tf_op jit(solution)/shard_map/dot_general | solution.py:51
  51.3 1.7 %copy-done.1 = f32[2048,384]{1,0:T(8,128)} copy-done((f32[2048,384]{1,0:T(8,128)}, f32[2048,384]{1,0:T(8,128)S(1)}, u32[]{:S(2)}) %copy-start.1) | copy-done | bytes 3145752
  53.2 2.5 %collective-permute-start.8 = (f32[384,1,128]{2,0,1:T(8,128)S(1)}, f32[384,1,128]{2,0,1:T(8,128)S(1)}, u32[]{:S(2)}, u32[]{:S(2)}) collective-permute-start(f32[384,1,128]{2,0,1:T(8,128)S(1)} %copy.57), channel_id=1, source_target_pairs={{4,0},{8,4},{12,8},{16,12},{20,16},{24,20},{28,24},{0,28},{5,1},{9... | collective-permute-start | bytes 589832 | tf_op jit(solution)/shard_map/ppermute | solution.py:33
  55.9 5.3 %copy.38 = f32[384,16,128]{0,1,2:T(8,128)} copy(f32[384,16,128]{0,2,1:T(8,128)} %bitcast.45) | data formatting | bytes 6291456 | tf_op jit(solution)/shard_map/reshape | solution.py:58
  61.2 0.2 copy.39
  61.4 2.2 %collective-permute-done.7 = f32[384,1,128]{2,0,1:T(8,128)S(1)} collective-permute-done((f32[384,1,128]{2,0,1:T(8,128)S(1)}, f32[384,1,128]{2,0,1:T(8,128)S(1)}, u32[]{:S(2)}, u32[]{:S(2)}) %collective-permute-start.7) | collective-permute-done | bytes 196640 | tf_op jit(solution)/shard_map/ppermute | solution.py:32
  63.6 0.2 copy.37
  63.8 2.6 %pad_maximum_fusion = f32[384,18,128]{0,1,2:T(8,128)S(1)} fusion(f32[384,1,128]{0,1,2:T(1,128)S(1)} %copy.39, f32[384,16,128]{0,1,2:T(8,128)} %copy.38, f32[384,1,128]{0,1,2:T(1,128)S(1)} %copy.37), kind=kLoop, calls=%fused_computation.11 | loop fusion | flops 1769472 | bytes 7077888 | tf_op jit(solution)/shard_map/concatenate | solution.py:34
  66.4 4.4 %collective-permute-start.10 = (f32[384,18,1]{0,1,2:T(8,128)S(1)}, f32[384,18,1]{0,1,2:T(8,128)S(1)}, u32[]{:S(2)}, u32[]{:S(2)}) collective-permute-start(f32[384,18,1]{0,1,2:T(8,128)S(1)} %get-tuple-element.61), channel_id=1, source_target_pairs={{1,0},{2,1},{3,2},{5,4},{6,5},{7,6},{9,8},{10,9},{11,10},{13,12},{... | collective-permute-start | bytes 82952 | tf_op jit(solution)/shard_map/ppermute | solution.py:33
  70.7 3.2 %collective-permute-start.9 = (f32[384,18,1]{0,1,2:T(8,128)S(1)}, f32[384,18,1]{0,1,2:T(8,128)S(1)}, u32[]{:S(2)}, u32[]{:S(2)}) collective-permute-start(f32[384,18,1]{0,1,2:T(8,128)S(1)} %get-tuple-element.60), channel_id=1, source_target_pairs={{0,1},{1,2},{2,3},{4,5},{5,6},{6,7},{8,9},{9,10},{10,11},{12,13},{... | collective-permute-start | bytes 82952 | tf_op jit(solution)/shard_map/ppermute | solution.py:32
  74.0 2.4 %copy.41 = f32[384,18,128]{0,2,1:T(8,128)} copy(f32[384,18,128]{0,1,2:T(8,128)S(1)} %pad_maximum_fusion) | data formatting | bytes 7077888 | tf_op jit(solution)/shard_map/concatenate | solution.py:34
  76.5 0.1 copy.34
  76.8 7.8 %fusion.16 = f32[384,16,128]{0,2,1:T(8,128)S(1)} fusion(f32[384,18,1]{0,2,1:T(1,128)S(1)} %copy.43, f32[384,18,128]{0,2,1:T(8,128)} %copy.41, f32[384,18,1]{0,2,1:T(1,128)S(1)} %copy.40, f32[384,1,128]{0,2,1:T(8,128)S(1)} %copy.36, f32[384,16,128]{0,2,1:T(8,128)} %bitcast.46, f32[384,1,128]{0,2,1:T(8,128)S(1)} %copy.34, f32[16,128]{1,0:T(8,128)S(1)} %get-tuple-element.68, ...), kind=kLoop, calls=%fused_computation.27 | loop fusion | flops 10223616 | bytes 10319872 | tf_op jit(solution)/shard_map/add | solution.py:40
  84.6 6.7 %fusion.35 = f32[2048,384]{1,0:T(8,128)S(1)} fusion(f32[384,2048]{0,1:T(8,128)S(1)} %bitcast.50, f32[384,384]{1,0:T(8,128)S(1)} %copy-done), kind=kOutput, calls=%fused_computation.69 | convolution fusion | flops 3623878656 | bytes 6881280 | tf_op jit(solution)/shard_map/dot_general | solution.py:51
  91.3 1.7 %copy-done.2 = f32[2048,384]{1,0:T(8,128)} copy-done((f32[2048,384]{1,0:T(8,128)}, f32[2048,384]{1,0:T(8,128)S(1)}, u32[]{:S(2)}) %copy-start.2) | copy-done | bytes 3145752
  93.1 2.3 %collective-permute-start.12 = (f32[384,1,128]{2,0,1:T(8,128)S(1)}, f32[384,1,128]{2,0,1:T(8,128)S(1)}, u32[]{:S(2)}, u32[]{:S(2)}) collective-permute-start(f32[384,1,128]{2,0,1:T(8,128)S(1)} %copy.59), channel_id=1, source_target_pairs={{4,0},{8,4},{12,8},{16,12},{20,16},{24,20},{28,24},{0,28},{5,1},{9... | collective-permute-start | bytes 589832 | tf_op jit(solution)/shard_map/ppermute | solution.py:33
  95.6 5.3 %copy.49 = f32[384,16,128]{0,1,2:T(8,128)} copy(f32[384,16,128]{0,2,1:T(8,128)} %bitcast.48) | data formatting | bytes 6291456 | tf_op jit(solution)/shard_map/reshape | solution.py:58
  101.0 0.2 copy.50
  101.1 3.9 %collective-permute-done.11 = f32[384,1,128]{2,0,1:T(8,128)S(1)} collective-permute-done((f32[384,1,128]{2,0,1:T(8,128)S(1)}, f32[384,1,128]{2,0,1:T(8,128)S(1)}, u32[]{:S(2)}, u32[]{:S(2)}) %collective-permute-start.11) | collective-permute-done | bytes 196640 | tf_op jit(solution)/shard_map/ppermute | solution.py:32
  105.1 0.2 copy.48
  105.2 2.6 %pad_maximum_fusion.1 = f32[384,18,128]{0,1,2:T(8,128)S(1)} fusion(f32[384,1,128]{0,1,2:T(1,128)S(1)} %copy.50, f32[384,16,128]{0,1,2:T(8,128)} %copy.49, f32[384,1,128]{0,1,2:T(1,128)S(1)} %copy.48), kind=kLoop, calls=%fused_computation.12 | loop fusion | flops 1769472 | bytes 7077888 | tf_op jit(solution)/shard_map/concatenate | solution.py:34
  107.8 2.5 %collective-permute-start.14 = (f32[384,18,1]{0,1,2:T(8,128)S(1)}, f32[384,18,1]{0,1,2:T(8,128)S(1)}, u32[]{:S(2)}, u32[]{:S(2)}) collective-permute-start(f32[384,18,1]{0,1,2:T(8,128)S(1)} %get-tuple-element.59), channel_id=1, source_target_pairs={{1,0},{2,1},{3,2},{5,4},{6,5},{7,6},{9,8},{10,9},{11,10},{13,12},{... | collective-permute-start | bytes 82952 | tf_op jit(solution)/shard_map/ppermute | solution.py:33
  110.3 3.1 %collective-permute-start.13 = (f32[384,18,1]{0,1,2:T(8,128)S(1)}, f32[384,18,1]{0,1,2:T(8,128)S(1)}, u32[]{:S(2)}, u32[]{:S(2)}) collective-permute-start(f32[384,18,1]{0,1,2:T(8,128)S(1)} %get-tuple-element.58), channel_id=1, source_target_pairs={{0,1},{1,2},{2,3},{4,5},{5,6},{6,7},{8,9},{9,10},{10,11},{12,13},{... | collective-permute-start | bytes 82952 | tf_op jit(solution)/shard_map/ppermute | solution.py:32
  113.4 2.4 %copy.52 = f32[384,18,128]{0,2,1:T(8,128)} copy(f32[384,18,128]{0,1,2:T(8,128)S(1)} %pad_maximum_fusion.1) | data formatting | bytes 7077888 | tf_op jit(solution)/shard_map/concatenate | solution.py:34
  115.9 0.1 copy.45
  116.2 9.0 %fusion.8 = f32[384,16,128]{0,2,1:T(8,128)} fusion(f32[384,18,1]{0,2,1:T(1,128)S(1)} %copy.54, f32[384,18,128]{0,2,1:T(8,128)} %copy.52, f32[384,18,1]{0,2,1:T(1,128)S(1)} %copy.51, f32[384,1,128]{0,2,1:T(8,128)S(1)} %copy.47, f32[384,16,128]{0,2,1:T(8,128)} %bitcast.49, f32[384,1,128]{0,2,1:T(8,128)S(1)} %copy.45, f32[16,128]{1,0:T(8,128)S(1)} %get-tuple-element.68, ...), kind=kLoop, calls=%fused_computation.15 | loop fusion | flops 10223616 | bytes 10319872 | tf_op jit(solution)/shard_map/add | solution.py:40
  125.1 3.5 %copy.55 = f32[384,16,128]{2,1,0:T(8,128)} copy(f32[384,16,128]{0,2,1:T(8,128)} %fusion.8) | data formatting | bytes 6291456 | tf_op jit(solution)/shard_map/add | solution.py:40
  (57 shorter events, 1.5 us)
Async XLA Ops:
  0.0 42.9 %copy-start = (f32[384,384]{1,0:T(8,128)S(1)}, f32[384,384]{1,0:T(8,128)}, u32[]{:S(2)}) copy-start(f32[384,384]{1,0:T(8,128)} %param.15) | copy-start | bytes 1769476
  0.0 15.2 %copy-start.5 = (s32[512]{0:T(512)S(1)}, s32[512]{0:T(512)}, u32[]{:S(2)}) copy-start(s32[512]{0:T(512)} %param.12) | copy-start | bytes 6148
  8.2 26.9 %all-to-all-start = ((bf16[8,128,384]{2,1,0:T(8,128)(2,1)}), bf16[8,128,384]{2,1,0:T(8,128)(2,1)S(1)}, u32[]{:S(2)}, u32[]{:S(2)}) async-start(bf16[8,128,384]{2,1,0:T(8,128)(2,1)} %bitcast.6), calls=%async_computation | async-start | bytes 1572864 | tf_op jit(solution)/shard_map/all_to_all | solution.py:85
  17.7 6.3 %collective-permute-start = (s32[1,128]{1,0:T(1,128)S(1)}, s32[1,128]{1,0:T(1,128)S(1)}, u32[]{:S(2)}, u32[]{:S(2)}) collective-permute-start(s32[1,128]{1,0:T(1,128)S(1)} %get-tuple-element.76), channel_id=1, source_target_pairs={{0,4},{4,0},{8,12},{12,8},{16,20},{20,16},{24,28},{28,24},{1,5},{5... | collective-permute-start | bytes 1544 | tf_op jit(solution)/shard_map/ppermute | solution.py:20
  19.3 7.8 %collective-permute-start.1 = (s32[1,128]{1,0:T(1,128)S(1)}, s32[1,128]{1,0:T(1,128)S(1)}, u32[]{:S(2)}, u32[]{:S(2)}) collective-permute-start(s32[1,128]{1,0:T(1,128)S(1)} %get-tuple-element.75), channel_id=1, source_target_pairs={{0,8},{4,12},{8,0},{12,4},{16,24},{20,28},{24,16},{28,20},{1,9},{5... | collective-permute-start | bytes 1544 | tf_op jit(solution)/shard_map/ppermute | solution.py:20
  20.5 10.4 %collective-permute-start.2 = (s32[1,128]{1,0:T(1,128)S(1)}, s32[1,128]{1,0:T(1,128)S(1)}, u32[]{:S(2)}, u32[]{:S(2)}) collective-permute-start(s32[1,128]{1,0:T(1,128)S(1)} %get-tuple-element.74), channel_id=1, source_target_pairs={{0,12},{4,8},{8,4},{12,0},{16,28},{20,24},{24,20},{28,16},{1,13},{... | collective-permute-start | bytes 1544 | tf_op jit(solution)/shard_map/ppermute | solution.py:20
  20.5 13.2 %collective-permute-start.3 = (s32[1,128]{1,0:T(1,128)S(1)}, s32[1,128]{1,0:T(1,128)S(1)}, u32[]{:S(2)}, u32[]{:S(2)}) collective-permute-start(s32[1,128]{1,0:T(1,128)S(1)} %get-tuple-element.73), channel_id=1, source_target_pairs={{0,16},{4,20},{8,24},{12,28},{16,0},{20,4},{24,8},{28,12},{1,17},{... | collective-permute-start | bytes 1544 | tf_op jit(solution)/shard_map/ppermute | solution.py:20
  22.8 12.0 %collective-permute-start.4 = (s32[1,128]{1,0:T(1,128)S(1)}, s32[1,128]{1,0:T(1,128)S(1)}, u32[]{:S(2)}, u32[]{:S(2)}) collective-permute-start(s32[1,128]{1,0:T(1,128)S(1)} %get-tuple-element.72), channel_id=1, source_target_pairs={{0,20},{4,16},{8,28},{12,24},{16,4},{20,0},{24,12},{28,8},{1,21},{... | collective-permute-start | bytes 1544 | tf_op jit(solution)/shard_map/ppermute | solution.py:20
  24.0 10.8 %collective-permute-start.5 = (s32[1,128]{1,0:T(1,128)S(1)}, s32[1,128]{1,0:T(1,128)S(1)}, u32[]{:S(2)}, u32[]{:S(2)}) collective-permute-start(s32[1,128]{1,0:T(1,128)S(1)} %get-tuple-element.71), channel_id=1, source_target_pairs={{0,24},{4,28},{8,16},{12,20},{16,8},{20,12},{24,0},{28,4},{1,25},{... | collective-permute-start | bytes 1544 | tf_op jit(solution)/shard_map/ppermute | solution.py:20
  27.1 7.8 %collective-permute-start.6 = (s32[1,128]{1,0:T(1,128)S(1)}, s32[1,128]{1,0:T(1,128)S(1)}, u32[]{:S(2)}, u32[]{:S(2)}) collective-permute-start(s32[1,128]{1,0:T(1,128)S(1)} %get-tuple-element.70), channel_id=1, source_target_pairs={{0,28},{4,24},{8,20},{12,16},{16,12},{20,8},{24,4},{28,0},{1,29},{... | collective-permute-start | bytes 1544 | tf_op jit(solution)/shard_map/ppermute | solution.py:20
  51.3 1.7 %copy-start.1 = (f32[2048,384]{1,0:T(8,128)}, f32[2048,384]{1,0:T(8,128)S(1)}, u32[]{:S(2)}) copy-start(f32[2048,384]{1,0:T(8,128)S(1)} %fusion.34) | copy-start | bytes 9437188
  53.2 8.1 %collective-permute-start.8 = (f32[384,1,128]{2,0,1:T(8,128)S(1)}, f32[384,1,128]{2,0,1:T(8,128)S(1)}, u32[]{:S(2)}, u32[]{:S(2)}) collective-permute-start(f32[384,1,128]{2,0,1:T(8,128)S(1)} %copy.57), channel_id=1, source_target_pairs={{4,0},{8,4},{12,8},{16,12},{20,16},{24,20},{28,24},{0,28},{5,1},{9... | collective-permute-start | bytes 589832 | tf_op jit(solution)/shard_map/ppermute | solution.py:33
  55.8 7.7 %collective-permute-start.7 = (f32[384,1,128]{2,0,1:T(8,128)S(1)}, f32[384,1,128]{2,0,1:T(8,128)S(1)}, u32[]{:S(2)}, u32[]{:S(2)}) collective-permute-start(f32[384,1,128]{2,0,1:T(8,128)S(1)} %copy.56), channel_id=1, source_target_pairs={{0,4},{4,8},{8,12},{12,16},{16,20},{20,24},{24,28},{28,0},{1,5},{5... | collective-permute-start | bytes 589832 | tf_op jit(solution)/shard_map/ppermute | solution.py:32
  63.7 10.2 %copy-start.4 = (f32[4,16,128]{2,1,0:T(8,128)S(1)}, f32[4,16,128]{2,1,0:T(8,128)}, u32[]{:S(2)}) copy-start(f32[4,16,128]{2,1,0:T(8,128)} %param.17) | copy-start | bytes 98308
  66.4 10.3 %collective-permute-start.10 = (f32[384,18,1]{0,1,2:T(8,128)S(1)}, f32[384,18,1]{0,1,2:T(8,128)S(1)}, u32[]{:S(2)}, u32[]{:S(2)}) collective-permute-start(f32[384,18,1]{0,1,2:T(8,128)S(1)} %get-tuple-element.61), channel_id=1, source_target_pairs={{1,0},{2,1},{3,2},{5,4},{6,5},{7,6},{9,8},{10,9},{11,10},{13,12},{... | collective-permute-start | bytes 82952 | tf_op jit(solution)/shard_map/ppermute | solution.py:33
  70.7 6.0 %collective-permute-start.9 = (f32[384,18,1]{0,1,2:T(8,128)S(1)}, f32[384,18,1]{0,1,2:T(8,128)S(1)}, u32[]{:S(2)}, u32[]{:S(2)}) collective-permute-start(f32[384,18,1]{0,1,2:T(8,128)S(1)} %get-tuple-element.60), channel_id=1, source_target_pairs={{0,1},{1,2},{2,3},{4,5},{5,6},{6,7},{8,9},{9,10},{10,11},{12,13},{... | collective-permute-start | bytes 82952 | tf_op jit(solution)/shard_map/ppermute | solution.py:32
  74.0 2.8 %copy-start.3 = (f32[16,128]{1,0:T(8,128)S(1)}, f32[16,128]{1,0:T(8,128)}, u32[]{:S(2)}) copy-start(f32[16,128]{1,0:T(8,128)} %param.16) | copy-start | bytes 24580
  91.3 1.7 %copy-start.2 = (f32[2048,384]{1,0:T(8,128)}, f32[2048,384]{1,0:T(8,128)S(1)}, u32[]{:S(2)}) copy-start(f32[2048,384]{1,0:T(8,128)S(1)} %fusion.35) | copy-start | bytes 9437188
  93.1 7.8 %collective-permute-start.12 = (f32[384,1,128]{2,0,1:T(8,128)S(1)}, f32[384,1,128]{2,0,1:T(8,128)S(1)}, u32[]{:S(2)}, u32[]{:S(2)}) collective-permute-start(f32[384,1,128]{2,0,1:T(8,128)S(1)} %copy.59), channel_id=1, source_target_pairs={{4,0},{8,4},{12,8},{16,12},{20,16},{24,20},{28,24},{0,28},{5,1},{9... | collective-permute-start | bytes 589832 | tf_op jit(solution)/shard_map/ppermute | solution.py:33
  95.5 9.5 %collective-permute-start.11 = (f32[384,1,128]{2,0,1:T(8,128)S(1)}, f32[384,1,128]{2,0,1:T(8,128)S(1)}, u32[]{:S(2)}, u32[]{:S(2)}) collective-permute-start(f32[384,1,128]{2,0,1:T(8,128)S(1)} %copy.58), channel_id=1, source_target_pairs={{0,4},{4,8},{8,12},{12,16},{16,20},{20,24},{24,28},{28,0},{1,5},{5... | collective-permute-start | bytes 589832 | tf_op jit(solution)/shard_map/ppermute | solution.py:32
  107.8 8.2 %collective-permute-start.14 = (f32[384,18,1]{0,1,2:T(8,128)S(1)}, f32[384,18,1]{0,1,2:T(8,128)S(1)}, u32[]{:S(2)}, u32[]{:S(2)}) collective-permute-start(f32[384,18,1]{0,1,2:T(8,128)S(1)} %get-tuple-element.59), channel_id=1, source_target_pairs={{1,0},{2,1},{3,2},{5,4},{6,5},{7,6},{9,8},{10,9},{11,10},{13,12},{... | collective-permute-start | bytes 82952 | tf_op jit(solution)/shard_map/ppermute | solution.py:33
  110.3 5.8 %collective-permute-start.13 = (f32[384,18,1]{0,1,2:T(8,128)S(1)}, f32[384,18,1]{0,1,2:T(8,128)S(1)}, u32[]{:S(2)}, u32[]{:S(2)}) collective-permute-start(f32[384,18,1]{0,1,2:T(8,128)S(1)} %get-tuple-element.58), channel_id=1, source_target_pairs={{0,1},{1,2},{2,3},{4,5},{5,6},{6,7},{8,9},{9,10},{10,11},{12,13},{... | collective-permute-start | bytes 82952 | tf_op jit(solution)/shard_map/ppermute | solution.py:32
